TPU v7x, 512 devices: a whole 4x4x16 slice. The times are simulated.
512 devices in a mesh: row: 16 (over z_hi, x, core), col: 32 (over z_lo, y).
Axes of the slice: x: 4, y: 4, z: 16 (z_hi: 2, z_lo: 8; z = z_hi * 8 + z_lo), core: 2. Of those that a mesh axis runs over, the one named last changes fastest.
Arguments:
- noisy_image: bfloat16 [512, 256, 256], P('row', 'col'), may hold values from -6 to 6
- time_index: int32 [1], replicated, may hold values from 0 to 31
- solver_index: int32 [1], replicated, may hold values from 0 to 31
- time_gains: float32 [32, 256], replicated, may hold values from 0.5 to 1.5
- pixel_qkv: bfloat16 [256, 768], replicated, may hold values from -0.375 to 0.375
- pixel_out: bfloat16 [256, 256], replicated, may hold values from -0.375 to 0.375
- coarse_gains: float32 [32, 1024], replicated, may hold values from 0.5 to 1.5
- coarse_qkv: bfloat16 [1024, 16, 192], P(None, 'row'), may hold values from -0.1875 to 0.1875
- coarse_out: bfloat16 [1024, 1024], P('row'), may hold values from -1.5 to 1.5
- upsample_weight: bfloat16 [1024, 1024], replicated, may hold values from -0.1875 to 0.1875
- skip_gain: float32 [256], replicated, may hold values from 0.5 to 1.5
- solver_table: float32 [32, 2], replicated, may hold values from 0.3 to 1
Outputs:
- next_image: float32 [512, 256, 256], P('row', 'col')
All inputs are finite; a program needn't handle non-finite values.
Results may differ from a plain program's by a relative error of at most 0.02.
Values may be sent and summed in bfloat16 or wider, within the bound.
A program may use at most 64 MiB of HBM per device.

v0:
```python
import math

import jax
import jax.numpy as jnp
from jax import lax
from jax.sharding import PartitionSpec as P

HEAD_DIM = 64
WINDOW = 7


def extended(block, sides, width):
    for axis, dim in sides:
        count = lax.axis_size(axis)
        forward = [(i, i + 1) for i in range(count - 1)]
        backward = [(target, source) for source, target in forward]
        low = lax.ppermute(
            lax.slice_in_dim(block, block.shape[dim] - width, None, axis=dim), axis, forward
        )
        high = lax.ppermute(lax.slice_in_dim(block, 0, width, axis=dim), axis, backward)
        block = jnp.concatenate([low, block, high], axis=dim)
    return block


def root_norm(values, scales):
    floats = values.astype(jnp.float32)
    factor = lax.rsqrt(jnp.mean(floats * floats, -1, keepdims=True) + 1e-06)
    return (floats * factor * scales).astype(jnp.bfloat16)


def window_attention(query, keys, values, inside):
    rows, cols = (query.shape[0], query.shape[1])
    query_f = query.astype(jnp.float32)
    score_list = []
    for shift_row in range(WINDOW):
        for shift_col in range(WINDOW):
            keyed = keys[shift_row : shift_row + rows, shift_col : shift_col + cols].astype(
                jnp.float32
            )
            scored = jnp.sum(query_f * keyed, -1) / math.sqrt(HEAD_DIM)
            usable = inside[shift_row : shift_row + rows, shift_col : shift_col + cols][:, :, None]
            score_list.append(jnp.where(usable, scored, -1e30))
    weights = jax.nn.softmax(jnp.stack(score_list, -1), -1).astype(jnp.bfloat16)
    total = jnp.zeros(query.shape, jnp.float32)
    for shift_row in range(WINDOW):
        for shift_col in range(WINDOW):
            offset = shift_row * WINDOW + shift_col
            valued = values[shift_row : shift_row + rows, shift_col : shift_col + cols].astype(
                jnp.float32
            )
            total = total + weights[..., offset, None].astype(jnp.float32) * valued
    return total.astype(jnp.bfloat16)


def shards(
    noisy_image,
    time_index,
    solver_index,
    time_gains,
    pixel_qkv,
    pixel_out,
    coarse_gains,
    coarse_qkv,
    coarse_out,
    upsample_weight,
    skip_gain,
    solver_table,
):
    tile_rows, tile_cols, width = noisy_image.shape
    pix_heads = width // HEAD_DIM
    coarse_width = 4 * width
    reach = WINDOW // 2
    row_count = lax.axis_size("row")
    col_count = lax.axis_size("col")
    pixel_scales = lax.dynamic_index_in_dim(time_gains, time_index[0], 0, False)
    normed = root_norm(noisy_image, pixel_scales)
    flattened = normed.reshape(tile_rows * tile_cols, width)
    query = jnp.dot(flattened, pixel_qkv[:, :width], preferred_element_type=jnp.float32)
    query = query.astype(jnp.bfloat16).reshape(tile_rows, tile_cols, pix_heads, HEAD_DIM)
    wide_rows, wide_cols = (tile_rows + 2 * reach, tile_cols + 2 * reach)
    local_pairs = jnp.dot(flattened, pixel_qkv[:, width:], preferred_element_type=jnp.float32)
    local_pairs = local_pairs.astype(jnp.bfloat16).reshape(tile_rows, tile_cols, 2 * width)
    key_values = extended(local_pairs, (("row", 0), ("col", 1)), reach)
    keys = key_values[..., :width].reshape(wide_rows, wide_cols, pix_heads, HEAD_DIM)
    values = key_values[..., width:].reshape(wide_rows, wide_cols, pix_heads, HEAD_DIM)
    row_place = lax.axis_index("row") * tile_rows + jnp.arange(wide_rows, dtype=jnp.int32) - reach
    col_place = lax.axis_index("col") * tile_cols + jnp.arange(wide_cols, dtype=jnp.int32) - reach
    row_inside = (row_place >= 0) & (row_place < tile_rows * row_count)
    col_inside = (col_place >= 0) & (col_place < tile_cols * col_count)
    inside = row_inside[:, None] & col_inside[None, :]
    attended = window_attention(query, keys, values, inside)
    mixed = jnp.dot(attended.reshape(-1, width), pixel_out, preferred_element_type=jnp.float32)
    pixels = (noisy_image.astype(jnp.float32) + mixed.reshape(tile_rows, tile_cols, width)).astype(
        jnp.bfloat16
    )
    half_rows, half_cols = (tile_rows // 2, tile_cols // 2)
    token_count = half_rows * half_cols
    merged = pixels.reshape(half_rows, 2, half_cols, 2, width).transpose(0, 2, 1, 3, 4)
    merged = merged.reshape(token_count, coarse_width)
    coarse_scales = lax.dynamic_index_in_dim(coarse_gains, time_index[0], 0, False)
    merged_normed = root_norm(merged, coarse_scales)
    local_heads = coarse_qkv.shape[1]
    result = jnp.einsum(
        "nc,chk->nhk",
        lax.all_gather(merged_normed, "row", axis=0, tiled=True),
        coarse_qkv,
        preferred_element_type=jnp.float32,
    )
    strip_proj = result.astype(jnp.bfloat16)
    strip_query = strip_proj[..., :HEAD_DIM]
    strip_keys = strip_proj[..., HEAD_DIM : 2 * HEAD_DIM]
    strip_values = strip_proj[..., 2 * HEAD_DIM :]
    scores = jnp.einsum("qhd,khd->hqk", strip_query, strip_keys, preferred_element_type=jnp.float32)
    weights = jax.nn.softmax(scores / math.sqrt(HEAD_DIM), -1).astype(jnp.bfloat16)
    outputs = jnp.einsum("hqk,khd->qhd", weights, strip_values, preferred_element_type=jnp.float32)
    outputs = outputs.astype(jnp.bfloat16)
    group_width = local_heads * HEAD_DIM
    flat_outputs = outputs.reshape(-1, group_width)
    delta = lax.psum_scatter(
        jnp.dot(flat_outputs, coarse_out, preferred_element_type=jnp.float32).astype(jnp.bfloat16),
        "row",
        scatter_dimension=0,
        tiled=True,
    ).astype(jnp.float32)
    coarse_next = (merged.astype(jnp.float32) + delta).astype(jnp.bfloat16)
    upsampled = jnp.dot(coarse_next, upsample_weight, preferred_element_type=jnp.float32)
    upsampled = upsampled.reshape(half_rows, half_cols, 2, 2, width).transpose(0, 2, 1, 3, 4)
    upsampled = upsampled.reshape(tile_rows, tile_cols, width)
    denoised = upsampled + skip_gain * pixels.astype(jnp.float32)
    coefficients = lax.dynamic_index_in_dim(solver_table, solver_index[0], 0, False)
    return coefficients[0] * noisy_image.astype(jnp.float32) + coefficients[1] * denoised


def solution(mesh):
    placed = (
        P("row", "col", None),
        P(),
        P(),
        P(),
        P(),
        P(),
        P(),
        P(None, "row", None),
        P("row", None),
        P(),
        P(),
        P(),
    )
    return jax.shard_map(
        shards, mesh=mesh, in_specs=placed, out_specs=P("row", "col", None), check_vma=False
    )
```

profile of v0, /device:TPU:9, one launch (start us, length us, event | category | flops | bytes accessed | tf_op | source)
XLA Modules:
  0.0 465.2 jit_solution(8618979284511567321)
XLA Ops:
  10.4 2.6 collective-permute-start.1
  13.0 3.0 collective-permute-start
  19.7 6.3 %collective-permute-start.3 = (bf16[38,3,512]{2,0,1:T(8,128)(2,1)}, bf16[38,3,512]{2,0,1:T(8,128)(2,1)S(1)}, u32[]{:S(2)}, u32[]{:S(2)}) collective-permute-start(bf16[38,3,512]{2,0,1:T(8,128)(2,1)} %get-tuple-element.106), channel_id=1, source_target_pairs={{1,0},{2,1},{3,2},{4,3},{5,4},{6,5},{7,6},{8,7},{9,8},{10,9},{11,1... | collective-permute-start | bytes 350216 | tf_op jit(solution)/shard_map/ppermute | solution.py:20
  26.0 1.9 collective-permute-start.2
  29.6 2.5 collective-permute-done.2
  35.1 5.0 %multiply_reduce_fusion.37 = (f32[32,8,4]{2,0,1:T(8,128)}, f32[32,8,4]{2,0,1:T(8,128)}, f32[32,8,4]{2,0,1:T(8,128)}, f32[32,8,4]{2,0,1:T(8,128)}, f32[32,8,4]{2,...) fusion(bf16[38,14,4,64]{3,2,0,1:T(4,128)(2,1)S(1)} %reshape.100, ...), kind=kLoop, calls=%fused_computation.57 | loop fusion | flops 2542592 | bytes 2019328 | tf_op jit(solution)/shard_map/reduce_sum | solution.py:40
  40.2 6.7 %multiply_reduce_fusion.19 = (f32[32,8,4]{2,0,1:T(8,128)}, f32[32,8,4]{2,0,1:T(8,128)}, f32[32,8,4]{2,0,1:T(8,128)}, f32[32,8,4]{2,0,1:T(8,128)}, f32[32,8,4]{2,...) fusion(bf16[38,14,4,64]{3,2,0,1:T(4,128)(2,1)S(1)} %reshape.100, ...), kind=kLoop, calls=%fused_computation.39 | loop fusion | flops 3520512 | bytes 2695168 | tf_op jit(solution)/shard_map/reduce_sum | solution.py:40
  46.8 6.8 %multiply_reduce_fusion.1 = (f32[32,8,4]{2,0,1:T(8,128)}, f32[32,8,4]{2,0,1:T(8,128)}, f32[32,8,4]{2,0,1:T(8,128)}, f32[32,8,4]{2,0,1:T(8,128)}, f32[32,8,4]{2,0...) fusion(bf16[38,14,4,64]{3,2,0,1:T(4,128)(2,1)S(1)} %reshape.100, ...), kind=kLoop, calls=%fused_computation.21 | loop fusion | flops 3520512 | bytes 2695168 | tf_op jit(solution)/shard_map/reduce_sum | solution.py:40
  60.9 1.6 copy.814
  65.8 1.6 copy.823
  67.4 1.6 copy.826
  70.7 1.6 copy.832
  75.5 1.6 copy.841
  82.0 1.6 copy.853
  93.3 1.6 copy.874
  96.6 1.6 copy.880
  114.4 1.6 copy.913
  208.7 16.1 %add_convert_fusion = bf16[32,8,4,64]{3,2,0,1:T(4,128)(2,1)S(1)} fusion(bf16[38,14,4,64]{3,2,0,1:T(4,128)(2,1)S(1)} %reshape.1006, f32[32,8,4]{2,0,1:T(8,128)S(1)} %copy.1031, f32[32,8,4]{2,0,1:T(8,128)S(1)} %copy.1030, f32[32,8,4]{2,0,1:T(8,128)S(1)} %copy.1029, f32[32,8,4]{2,0,1:T(8,128)} %copy.1028, f32[32,8,4]{2,0,1:T(8,128)} %copy.1027, ...), kind=kLoop, calls=%fused_computation.20 | loop fusion | flops 9633792 | bytes 6754304 | tf_op jit(solution)/shard_map/convert_element_type | solution.py:52
  228.2 104.0 %all-gather.2.cloned.1.call-done = bf16[1024,1024]{1,0:T(8,128)(2,1)} async-done(((bf16[64,1024]{1,0:T(8,128)(2,1)}), bf16[1024,1024]{1,0:T(8,128)(2,1)}) %all-gather.2.cloned.1.call-update) | async-done | bytes 2097168 | tf_op jit(solution)/shard_map/all_gather | solution.py:105
  332.2 2.5 fusion.2
  335.5 1.9 copy-done.1
  338.1 5.1 %convolution_convert_fusion = bf16[1024,1024]{1,0:T(8,128)(2,1)} fusion(bf16[64,1024]{1,0:T(8,128)(2,1)S(1)} %copy-done.13, f32[1024,1024]{0,1:T(8,128)} %copy-done.1, f32[1024]{0:T(1024)S(1)} %fusion, f32[1024]{0:T(1024)S(1)} %get-tuple-element.162, bf16[1024,1,192]{0,2,1:T(8,128)(2,1)S(1)} %fusion.2), kind=kOutput, calls=%fused_computation.5 | convolution fusion | flops 273743872 | bytes 6561792 | tf_op jit(solution)/shard_map/dot_general | solution.py:120
  344.6 109.9 %reduce-scatter.2.cloned.1.call-done = bf16[64,1024]{1,0:T(8,128)(2,1)} async-done(((bf16[1024,1024]{1,0:T(8,128)(2,1)}), bf16[64,1024]{1,0:T(8,128)(2,1)}) %reduce-scatter.2.cloned.1.call-update) | async-done | bytes 131088 | tf_op jit(solution)/shard_map/reduce_scatter | solution.py:119
  456.3 2.0 fusion.10
  (220 shorter events, 158.9 us)
Async XLA Ops:
  6.5 448.0 %copy-start = (bf16[1024,1024]{1,0:T(8,128)(2,1)S(1)}, bf16[1024,1024]{1,0:T(8,128)(2,1)}, u32[]{:S(2)}) copy-start(bf16[1024,1024]{1,0:T(8,128)(2,1)} %param.21) | copy-start | bytes 6291460
  6.5 325.7 %all-gather.2.cloned.1.call-start = ((), (), s32[]{:S(2)}) async-start(), calls=%async_computation.1 | async-start | bytes 2228224 | tf_op jit(solution)/shard_map/all_gather | solution.py:105
  10.4 8.5 %collective-permute-start.1 = (bf16[3,8,512]{2,0,1:T(4,128)(2,1)S(1)}, bf16[3,8,512]{2,0,1:T(4,128)(2,1)S(1)}, u32[]{:S(2)}, u32[]{:S(2)}) collective-permute-start(bf16[3,8,512]{2,0,1:T(4,128)(2,1)S(1)} %copy.790), channel_id=1, source_target_pairs={{32,0},{64,32},{96,64},{128,96},{160,128},{192,160},{224,192},{256... | collective-permute-start | bytes 73736 | tf_op jit(solution)/shard_map/ppermute | solution.py:20
  13.0 5.9 %collective-permute-start = (bf16[3,8,512]{2,0,1:T(4,128)(2,1)S(1)}, bf16[3,8,512]{2,0,1:T(4,128)(2,1)S(1)}, u32[]{:S(2)}, u32[]{:S(2)}) collective-permute-start(bf16[3,8,512]{2,0,1:T(4,128)(2,1)S(1)} %copy.789), channel_id=1, source_target_pairs={{0,32},{32,64},{64,96},{96,128},{128,160},{160,192},{192,224},{224... | collective-permute-start | bytes 73736 | tf_op jit(solution)/shard_map/ppermute | solution.py:17
  19.7 10.0 %collective-permute-start.3 = (bf16[38,3,512]{2,0,1:T(8,128)(2,1)}, bf16[38,3,512]{2,0,1:T(8,128)(2,1)S(1)}, u32[]{:S(2)}, u32[]{:S(2)}) collective-permute-start(bf16[38,3,512]{2,0,1:T(8,128)(2,1)} %get-tuple-element.106), channel_id=1, source_target_pairs={{1,0},{2,1},{3,2},{4,3},{5,4},{6,5},{7,6},{8,7},{9,8},{10,9},{11,1... | collective-permute-start | bytes 350216 | tf_op jit(solution)/shard_map/ppermute | solution.py:20
  26.0 6.1 %collective-permute-start.2 = (bf16[38,3,512]{2,0,1:T(8,128)(2,1)S(1)}, bf16[38,3,512]{2,0,1:T(8,128)(2,1)}, u32[]{:S(2)}, u32[]{:S(2)}) collective-permute-start(bf16[38,3,512]{2,0,1:T(8,128)(2,1)S(1)} %get-tuple-element.105), channel_id=1, source_target_pairs={{0,1},{1,2},{2,3},{3,4},{4,5},{5,6},{6,7},{7,8},{8,9},{9,10},{10,1... | collective-permute-start | bytes 350216 | tf_op jit(solution)/shard_map/ppermute | solution.py:17
  53.6 62.4 %copy-start.10 = (f32[32,8,4]{2,0,1:T(8,128)S(1)}, f32[32,8,4]{2,0,1:T(8,128)}, u32[]{:S(2)}) copy-start(f32[32,8,4]{2,0,1:T(8,128)} %get-tuple-element.12) | copy-start | bytes 12292
  53.6 63.1 %copy-start.9 = (f32[32,8,4]{2,0,1:T(8,128)S(1)}, f32[32,8,4]{2,0,1:T(8,128)}, u32[]{:S(2)}) copy-start(f32[32,8,4]{2,0,1:T(8,128)} %get-tuple-element.11) | copy-start | bytes 12292
  53.6 63.2 %copy-start.8 = (f32[32,8,4]{2,0,1:T(8,128)S(1)}, f32[32,8,4]{2,0,1:T(8,128)}, u32[]{:S(2)}) copy-start(f32[32,8,4]{2,0,1:T(8,128)} %get-tuple-element.10) | copy-start | bytes 12292
  53.6 63.3 %copy-start.7 = (f32[32,8,4]{2,0,1:T(8,128)S(1)}, f32[32,8,4]{2,0,1:T(8,128)}, u32[]{:S(2)}) copy-start(f32[32,8,4]{2,0,1:T(8,128)} %get-tuple-element.9) | copy-start | bytes 12292
  53.6 63.5 %copy-start.6 = (f32[32,8,4]{2,0,1:T(8,128)S(1)}, f32[32,8,4]{2,0,1:T(8,128)}, u32[]{:S(2)}) copy-start(f32[32,8,4]{2,0,1:T(8,128)} %get-tuple-element.8) | copy-start | bytes 12292
  53.6 63.6 %copy-start.5 = (f32[32,8,4]{2,0,1:T(8,128)S(1)}, f32[32,8,4]{2,0,1:T(8,128)}, u32[]{:S(2)}) copy-start(f32[32,8,4]{2,0,1:T(8,128)} %get-tuple-element.7) | copy-start | bytes 12292
  53.6 63.7 %copy-start.4 = (f32[32,8,4]{2,0,1:T(8,128)S(1)}, f32[32,8,4]{2,0,1:T(8,128)}, u32[]{:S(2)}) copy-start(f32[32,8,4]{2,0,1:T(8,128)} %get-tuple-element.6) | copy-start | bytes 12292
  53.7 63.8 %copy-start.3 = (f32[32,8,4]{2,0,1:T(8,128)S(1)}, f32[32,8,4]{2,0,1:T(8,128)}, u32[]{:S(2)}) copy-start(f32[32,8,4]{2,0,1:T(8,128)} %get-tuple-element.5) | copy-start | bytes 12292
  208.7 16.4 %copy-start.2 = (bf16[32,8,256]{2,1,0:T(8,128)(2,1)S(1)}, bf16[32,8,256]{2,1,0:T(8,128)(2,1)}, u32[]{:S(2)}) copy-start(bf16[32,8,256]{2,1,0:T(8,128)(2,1)} %param.12) | copy-start | bytes 393220
  227.9 226.6 %reduce-scatter.2.cloned.1.call-start = ((), (), s32[]{:S(2)}) async-start(), calls=%async_computation.2 | async-start | bytes 2228224 | tf_op jit(solution)/shard_map/reduce_scatter | solution.py:119
  334.7 3.4 copy-start.13
  335.5 1.9 copy-start.1
  338.1 5.8 %copy-start.12 = (f32[32,2]{0,1:T(2,128)S(1)}, f32[32,2]{0,1:T(2,128)}, u32[]{:S(2)}) copy-start(f32[32,2]{0,1:T(2,128)} %param.23) | copy-start | bytes 772
  343.2 113.1 %copy-start.11 = (f32[256]{0:T(256)S(1)}, f32[256]{0:T(256)}, u32[]{:S(2)}) copy-start(f32[256]{0:T(256)} %param.22) | copy-start | bytes 3076
Sparse Core Ops, SparseCore 0:
  228.0 104.1 all-gather.1
  343.4 111.0 reduce-scatter.1
where the time goes:
time: 473 us; the launch traced here: 465 us
  waiting for transfers between devices  216 us (46%)
  local copies, waits for them, and re-layouts  128 us (27%)
  other arithmetic  77.9 us (16%)
  between operations  15.3 us (3%)
  starting transfers between devices  14.1 us (3%)
  matrix products  13.4 us (3%)
    reduce_scatter x1, waiting for transfers between devices, shards(): lax.psum_scatter(jnp.dot(flat_outputs, coarse_out, preferred_element_type...  110 us
    all_gather x1, waiting for transfers between devices, shards(): lax.all_gather(merged_normed, 'row', axis=0, tiled=True)  104 us
    reduce_sum x49, local copies, waits for them, and re-layouts, window_attention(): scored = jnp.sum(query_f * keyed, -1) / math.sqrt(HEAD_DIM)  63.9 us
    mul x49, local copies, waits for them, and re-layouts, window_attention(): total = total + weights[..., offset, None].astype(jnp.float32) * valued  53.9 us
    unnamed x48, other arithmetic  33.9 us
    reduce_sum x3, other arithmetic, window_attention(): scored = jnp.sum(query_f * keyed, -1) / math.sqrt(HEAD_DIM)  18.5 us
    convert_element_type x1, other arithmetic, window_attention(): return total.astype(jnp.bfloat16)  16.1 us
  transfers between devices with their start and end apart: 6, of which 3 were waited for; matrix products, arithmetic and copies ran while one was open for 1% of the time, Pallas kernels for 0%

commit v1 on v0

v1 whole, which is shorter than its diff:
```python
import jax
import jax.numpy as jnp
from jax import lax
from jax.experimental import pallas as pl
from jax.experimental.pallas import tpu as pltpu
from jax.sharding import PartitionSpec as P

MESH = pl.DeviceIdType.MESH
BF = jnp.bfloat16
F32 = jnp.float32
ROWS, COLS = 16, 32
TOKENS = 64
WIDE = 1024
CHUNKS = 4
PER = TOKENS // CHUNKS
DIRS = ((-1, 0), (1, 0), (0, -1), (0, 1), (-1, -1), (-1, 1), (1, -1), (1, 1))


def iota(shape, dim):
    return lax.broadcasted_iota(jnp.int32, shape, dim)


def nt(left, right):
    return lax.dot_general(left, right, (((1,), (1,)), ((), ())), preferred_element_type=F32)


def mm(left, right):
    return jnp.dot(left, right, preferred_element_type=F32)


def norm(floats, scales):
    factor = lax.rsqrt(jnp.mean(floats * floats, -1, keepdims=True) + 1e-06)
    return (floats * factor * scales).astype(BF)


def pick(table, index):
    hit = iota(table.shape, 0) == index
    return jnp.sum(jnp.where(hit, table, 0.0), 0, keepdims=True)


def kernel(
    time_ref,
    step_ref,
    noisy_hbm,
    solver_hbm,
    gains_hbm,
    qkv_hbm,
    pout_hbm,
    cgains_hbm,
    skip_hbm,
    cqkv_hbm,
    cout_hbm,
    up_hbm,
    out_ref,
    noisy_ref,
    solver_ref,
    gains_ref,
    qkv_ref,
    pout_ref,
    cgains_ref,
    skip_ref,
    cc,
    ll,
    rr,
    pack_l,
    pack_r,
    kv_c,
    kv_e,
    query,
    noisy_m,
    merged,
    own,
    tok,
    wt,
    w3,
    wo,
    wup,
    asked_all,
    keys_all,
    values_all,
    ret_s,
    ret_r,
    halo_s,
    halo_r,
    z_s,
    z_r,
    xr_s,
    xr_r,
    xl_s,
    xl_r,
    xf_s,
    xf_r,
    sib_s,
    sib_r,
    w1_s,
    w1_r,
    wx_s,
    wx_r,
    w2_s,
    w2_r,
    w3_s,
    w3_r,
    w4_s,
    w4_r,
    back_s,
    back_r,
    local,
):
    row, col = lax.axis_index("row"), lax.axis_index("col")
    half, xx, core = row // 8, (row // 2) % 4, row % 2
    yy = col % 4
    group = row // 2
    far_col = jnp.where(col >= 16, col - 16, col + 16)
    far_row = jnp.where(row >= 8, row - 8, row + 8)
    sibling = row + 1 - 2 * core

    fourth = jnp.where(row == 8, 0, 3)
    third = 3 - fourth

    def x_row(shift):
        return half * 8 + ((xx + shift) % 4) * 2 + core

    def y_col(shift):
        return col - yy + (yy + shift) % 4

    def remote(src, dst, send, recv, where):
        return pltpu.make_async_remote_copy(
            src_ref=src, dst_ref=dst, send_sem=send, recv_sem=recv, device_id=where, device_id_type=MESH
        )

    def arrive(dst, recv, send):
        remote(dst, dst, send, recv, (row, col)).wait_recv()

    sent = []

    def send(*args):
        remote(*args).start()

    def sent_by(sem, ref):
        sent.append((sem, ref))

    def wait_sent():
        for sem, ref in sent:
            remote(ref, ref, sem, local.at[0], (row, col)).wait_send()
        sent.clear()

    def load(src, dst, at):
        copy = pltpu.make_async_copy(src, dst, local.at[at])
        copy.start()
        return copy

    load_noisy = load(noisy_hbm, noisy_ref, 3)

    barrier = pltpu.get_barrier_semaphore()

    def greet(where):
        pl.semaphore_signal(barrier, inc=1, device_id=where, device_id_type=MESH)

    there = []
    for down, right in DIRS:
        r, c = row + down, col + right
        there.append((r >= 0) & (r < ROWS) & (c >= 0) & (c < COLS))
    for d, (down, right) in enumerate(DIRS):

        @pl.when(there[d])
        def _():
            greet((row + down, col + right))

    greet((row, far_col))
    greet((far_row, far_col))
    for shift in (1, 2, 3):
        greet((x_row(shift), col))
        greet((row, y_col(shift)))
    greet((sibling, col))
    partners = 2 + 6 + 1
    for flag in there:
        partners = partners + flag.astype(jnp.int32)

    quarter = pl.ds(pl.multiple_of(yy * 16, 16), 16)
    own_quarter = wo.at[group, core, quarter]
    quarter = pl.ds(pl.multiple_of(yy * 16, 16), 16)
    own_quarter = wo.at[group, core, quarter]
    own_block = wo.at[group, core]
    load_wo = load(cout_hbm, own_block, 0)
    load_gains = load(gains_hbm, gains_ref, 4)
    load_qkv = load(qkv_hbm, qkv_ref, 5)
    load_pout = load(pout_hbm, pout_ref, 6)
    load_cgains = load(cgains_hbm, cgains_ref, 7)
    load_wt = load(cqkv_hbm, wt, 1)
    load_skip = load(skip_hbm, skip_ref, 8)
    load_solver = load(solver_hbm, solver_ref, 9)
    load_up = load(up_hbm, wup, 2)

    load_noisy.wait()
    tile = noisy_ref[...].astype(F32).reshape(256, 256)
    tile_b = tile.astype(BF)
    cc[32:288, :] = tile_b
    spot = iota((128, 256), 0)
    place = (spot >> 2) * 8 + (spot & 3)
    lane = iota((128, 256), 1)
    pack_l[...] = mm((lane == place).astype(F32).astype(BF), tile_b).astype(BF)
    pack_r[...] = mm((lane == place + 4).astype(F32).astype(BF), tile_b).astype(BF)

    pl.semaphore_wait(barrier, partners)

    halo = (
        (cc.at[32:64], cc.at[288:320]),
        (cc.at[256:288], cc.at[0:32]),
        (pack_l, rr.at[16:144]),
        (pack_r, ll.at[16:144]),
        (pack_l.at[0:16], rr.at[144:160]),
        (pack_r.at[0:16], ll.at[144:160]),
        (pack_l.at[112:128], rr.at[0:16]),
        (pack_r.at[112:128], ll.at[0:16]),
    )

    def halo_copy(d):
        src, dst = halo[d]
        return remote(src, dst, halo_s.at[d], halo_r.at[d], (row + DIRS[d][0], col + DIRS[d][1]))

    for d in (2, 3, 0, 1, 4, 5, 6, 7):

        @pl.when(there[d])
        def _():
            halo_copy(d).start()

    from_there = []
    for down, right in DIRS:
        r, c = row - down, col - right
        from_there.append((r >= 0) & (r < ROWS) & (c >= 0) & (c < COLS))
    for d in range(8):

        @pl.when(jnp.logical_not(from_there[d]))
        def _():
            dst = halo[d][1]
            dst[...] = jnp.zeros(dst.shape, BF)

    load_wo.wait()
    send(own_quarter, own_quarter, w1_s.at[0], w1_r.at[0], (far_row, far_col))
    sent_by(w1_s.at[0], own_quarter)
    for shift in (1, 2, 3):
        send(own_block, own_block, wx_s.at[0], wx_r.at[0], (x_row(shift), col))
    three = pl.ds(0, 3)
    sent_by(wx_s.at[0], wo.at[three, core])

    load_gains.wait()
    scales = pick(gains_ref[...], time_ref[0])
    normed = norm(tile, scales)
    load_qkv.wait()
    kv_c[32:288, :] = mm(normed, qkv_ref[:, 256:768]).astype(BF)
    i = iota((256, 256), 0)
    spot, a, b, p, q = i >> 6, (i >> 5) & 1, (i >> 4) & 1, (i >> 2) & 3, i & 3
    blk = jnp.where(spot < 2, spot + 1, jnp.where(spot == 2, third, fourth))
    source = (8 * blk + 2 * p + a) * 8 + 2 * q + b
    shuffle = (iota((256, 256), 1) == source).astype(F32).astype(BF)
    noisy_q = mm(shuffle, tile_b)
    normed_q = mm(shuffle, normed).astype(BF)
    query[...] = mm(normed_q, qkv_ref[:, 0:256]).astype(BF)
    noisy_qb = noisy_q.astype(BF)
    for block in range(4):
        for ab in range(4):
            at = block * 64 + ab * 16
            noisy_m[block * 16 : block * 16 + 16, ab * 256 : ab * 256 + 256] = noisy_qb[at : at + 16]

    load_wt.wait()
    w3[0:64, :] = (wt[0:64, :].astype(F32) * 0.125).astype(BF)
    w3[64:192, :] = wt[64:192, :]
    w3[192:256, :] = jnp.zeros((64, WIDE), BF)

    def halo_wait(d, flag):
        @pl.when(from_there[d] & flag)
        def _():
            arrive(halo[d][1], halo_r.at[d], halo_s.at[d])

    def edge_kv(array):
        return mm(norm(array.astype(F32), scales), qkv_ref[:, 256:768]).astype(BF)

    halo_wait(2, True)
    halo_wait(3, True)
    sides = edge_kv(jnp.concatenate([ll[16:144, :], rr[16:144, :]], 0))
    kv_e[16:144, :] = sides[0:128]
    kv_e[176:304, :] = sides[128:256]

    def outer_edge(block, last):
        above = (row == 8) if last else (row != 8)
        for d in (1, 6, 7):
            halo_wait(d, above)
        for d in (0, 4, 5):
            halo_wait(d, jnp.logical_not(above))
        wide = pl.ds(pl.multiple_of(jnp.where(block == 0, 0, 288), 32), 32)
        start = jnp.where(block == 0, 0, 144)
        narrow = pl.ds(pl.multiple_of(start, 16), 16)
        result = edge_kv(jnp.concatenate([cc[wide, :], ll[narrow, :], rr[narrow, :]], 0))
        kv_c[wide, :] = result[0:32]
        kv_e[narrow, :] = result[32:48]
        kv_e[pl.ds(pl.multiple_of(160 + start, 16), 16), :] = result[48:64]

    j = iota((64, 256), 1)
    in_c = j < 128
    key_row = jnp.where(in_c, j >> 3, (j & 63) >> 2) - 4
    key_col = jnp.where(in_c, j & 7, (j & 3) + jnp.where(j < 192, -4, 8))
    i = iota((64, 256), 0)
    query_row = 2 * ((i >> 2) & 3) + ((i >> 5) & 1)
    query_col = 2 * (i & 3) + ((i >> 4) & 1)
    full_col = key_col + col * 8
    near = (
        (jnp.abs(key_row - query_row) <= 3)
        & (jnp.abs(key_col - query_col) <= 3)
        & (full_col >= 0)
        & (full_col < 256)
    )
    head_of = iota((64, 256), 1) >> 6
    ones = jnp.ones((256, 256), BF)
    load_cgains.wait()
    load_pout.wait()
    coarse_scales = pick(cgains_ref[...], time_ref[0])

    def window_block(spot, block):
        inner = pl.ds(pl.multiple_of(64 * block, 64), 128)
        lefts = pl.ds(pl.multiple_of(32 * block, 32), 64)
        rights = pl.ds(pl.multiple_of(160 + 32 * block, 32), 64)
        keys = jnp.concatenate([kv_c[inner, 0:256], kv_e[lefts, 0:256], kv_e[rights, 0:256]], 0)
        values = jnp.concatenate([kv_c[inner, 256:512], kv_e[lefts, 256:512], kv_e[rights, 256:512]], 0)
        asked = query[64 * spot : 64 * spot + 64, :].astype(F32) * 0.125
        spread = jnp.concatenate([jnp.where(head_of == h, asked, 0.0) for h in range(4)], 0).astype(BF)
        full_row = key_row + (row * 32 + 8 * block)
        usable = near & (full_row >= 0) & (full_row < 512)
        bias = jnp.where(usable, 0.0, -1e30)
        scores = nt(spread, keys) + jnp.concatenate([bias] * 4, 0)
        weights = jnp.exp(scores - jnp.max(scores, 1, keepdims=True)).astype(BF)
        sums = mm(weights, ones)
        mixed = mm(weights, values)
        total, share = jnp.zeros((64, 256), F32), jnp.zeros((64, 256), F32)
        for h in range(4):
            total = jnp.where(head_of == h, sums[64 * h : 64 * h + 64], total)
            share = jnp.where(head_of == h, mixed[64 * h : 64 * h + 64], share)
        attended = (share / total).astype(BF)
        delta = mm(attended, pout_ref[...])
        for ab in range(4):
            rows, lanes = pl.ds(spot * 16, 16), pl.ds(ab * 256, 256)
            pixels = noisy_m[rows, lanes].astype(F32) + delta[ab * 16 : ab * 16 + 16]
            merged[rows, lanes] = pixels.astype(BF)

    def part(k):
        return pl.ds(k * PER, PER)

    for k in range(CHUNKS):
        if k < 2:
            window_block(k, k + 1)
        else:
            outer_edge(third if k == 2 else fourth, k == 3)
            window_block(k, third if k == 2 else fourth)
        own[part(k), :] = norm(merged[part(k), :].astype(F32), coarse_scales)
        for t, target in enumerate((row, far_row)):
            send(
                own.at[part(k)],
                tok.at[half, xx, core, part(k)],
                z_s.at[t],
                z_r.at[k],
                (target, far_col),
            )
    for t in range(2):
        sent_by(z_s.at[t], own)

    near_blocks = pl.ds(pl.multiple_of(half * 4, 4), 4)
    far_blocks = pl.ds(pl.multiple_of(4 - half * 4, 4), 4)

    def weights_x():
        ref = wo.at[far_row // 2, core, quarter]
        arrive(ref, w1_r.at[0], w1_s.at[0])
        for shift in (1, 2, 3):
            send(ref, ref, w2_s.at[0], w2_r.at[0], (x_row(shift), col))
        sent_by(w2_s.at[0], wo.at[three, core, quarter])

    def weights_y():
        arrive(wo.at[three, core, quarter], w2_r.at[0], w2_s.at[0])
        ref = wo.at[far_blocks, core, quarter]
        for shift in (1, 2, 3):
            send(ref, ref, w3_s.at[0], w3_r.at[0], (row, y_col(shift)))
        sent_by(w3_s.at[0], wo.at[far_blocks, core, pl.ds(0, 48)])

    def weights_near():
        arrive(wo.at[three, core], wx_r.at[0], wx_s.at[0])
        ref = wo.at[near_blocks, core]
        send(ref, ref, w4_s.at[0], w4_r.at[0], (sibling, col))
        sent_by(w4_s.at[0], ref)

    def weights_far():
        arrive(wo.at[far_blocks, core, pl.ds(0, 48)], w3_r.at[0], w3_s.at[0])
        ref = wo.at[far_blocks, core]
        send(ref, ref, w4_s.at[1], w4_r.at[1], (sibling, col))
        sent_by(w4_s.at[1], ref)

    def blocks(shift, k, which=core):
        return tok.at[:, (xx + shift) % 4, which, part(k)]

    def one(side, shift, k):
        return tok.at[side, (xx + shift) % 4, core, part(k)]

    def to_sibling(shift, k):
        ref = blocks(shift, k)
        send(ref, ref, sib_s.at[0], sib_r.at[k], (sibling, col))

    def gather(k):
        ref = blocks(0, k)
        arrive(ref, z_r.at[k], z_s.at[0])
        send(ref, ref, xr_s.at[0], xr_r.at[k], (x_row(1), col))
        send(ref, ref, xl_s.at[0], xl_r.at[k], (x_row(3), col))
        to_sibling(0, k)

    def relay(k):
        arrive(blocks(3, k), xr_r.at[k], xr_s.at[0])
        ref = one(0, 3, k)
        send(ref, ref, xf_s.at[0], xf_r.at[k], (x_row(1), col))
        to_sibling(3, k)
        arrive(blocks(1, k), xl_r.at[k], xl_s.at[0])
        ref = one(1, 1, k)
        send(ref, ref, xf_s.at[1], xf_r.at[k], (x_row(3), col))
        to_sibling(1, k)

    def finish(k):
        arrive(blocks(2, k), xf_r.at[k], xf_s.at[0])
        to_sibling(2, k)

    def from_sibling(k):
        arrive(tok.at[:, :, 1 - core, part(k)], sib_r.at[k], sib_s.at[0])

    left = iota((16 * PER, 128), 1) < 64

    def project(k):
        tokens = tok[:, :, :, k * PER : (k + 1) * PER, :].reshape(16 * PER, WIDE)
        result = nt(tokens, w3[...])
        both, value = result[:, 0:128], result[:, 128:256]
        for ref, array in (
            (asked_all, jnp.where(left, both, 0.0)),
            (keys_all, pltpu.roll(both, 64, 1)),
            (values_all, jnp.where(left, value, 1.0)),
        ):
            ref[:, :, :, k * PER : (k + 1) * PER, :] = array.astype(BF).reshape(2, 4, 2, PER, 128)

    weights_x()
    gather(0)
    weights_y()
    relay(0)
    for k in range(1, CHUNKS):
        gather(k)
        finish(k - 1)
        relay(k)
        if k == 2:
            weights_near()
        from_sibling(k - 1)
        project(k - 1)
    finish(CHUNKS - 1)
    from_sibling(CHUNKS - 1)
    project(CHUNKS - 1)

    low = iota((32, 128), 1) < 64
    keys = keys_all[...].reshape(WIDE, 128)
    values = values_all[...].reshape(WIDE, 128)

    turns = (2, 1, 3, 0)

    def score(turn):
        return nt(asked_all[:, (xx + turns[turn]) % 4].reshape(256, 128), keys)

    whole = tok.at[:, xx, core]
    for sem in (xr_s.at[0], xl_s.at[0]):
        sent_by(sem, whole)
    for side in range(2):
        sent_by(xf_s.at[side], tok.at[side, xx, core])
    sent_by(sib_s.at[0], tok.at[:, :, core])

    scores = score(0)
    for turn in range(4):
        following = score(turn + 1) if turn < 3 else None
        weights = jnp.exp(scores - jnp.max(scores, 1, keepdims=True)).astype(BF)
        mixed = mm(weights, values)
        mixed = mixed / pltpu.roll(mixed, 64, 1)
        for which in range(4):
            at = 64 * which
            packed = jnp.where(low, mixed[at : at + 32], pltpu.roll(mixed[at + 32 : at + 64], 64, 1))
            ret_s[turn, which] = packed.astype(BF)
        for which in range(4):
            target = (which // 2) * 8 + ((xx + turns[turn]) % 4) * 2 + which % 2
            send(
                ret_s.at[turn, which],
                ret_r.at[turn, 2 * half + core],
                back_s.at[0],
                back_r.at[turn],
                (target, far_col),
            )
        scores = following

    weights_far()

    load_up.wait()
    load_skip.wait()
    load_solver.wait()
    pixels = merged[...].astype(F32)
    table = solver_ref[...]
    table = jnp.where(iota(table.shape, 1) == step_ref[0], table, 0.0)
    keep = jnp.sum(table[0:1], 1, keepdims=True)
    gain = jnp.sum(table[1:2], 1, keepdims=True)
    skip = skip_ref[...].reshape(1, 256)
    base = keep * noisy_m[...].astype(F32) + gain * (jnp.concatenate([skip] * 4, 1) * pixels)
    i = iota((256, 256), 0)
    r, c = i >> 3, i & 7
    block = r >> 3
    spot = jnp.where((block == 1) | (block == 2), block - 1, jnp.where(block == third, 2, 3))
    source = (2 * (r & 1) + (c & 1)) * 64 + spot * 16 + ((r >> 1) & 3) * 4 + (c >> 1)
    unshuffle = (iota((256, 256), 1) == source).astype(F32).astype(BF)
    arrive(wo.at[near_blocks, 1 - core], w4_r.at[0], w4_s.at[0])
    arrive(wo.at[far_blocks, 1 - core], w4_r.at[1], w4_s.at[1])
    for d in range(8):

        @pl.when(there[d])
        def _():
            halo_copy(d).wait_send()

    wait_sent()

    coarse_next = pixels
    for turn in range(4):
        arrive(ret_r.at[turn], back_r.at[turn], back_s.at[0])
        first, second, weight = [], [], []
        for side in range(2):
            even, odd = ret_r[turn, 2 * side].astype(F32), ret_r[turn, 2 * side + 1].astype(F32)
            first.append(jnp.where(low, even, pltpu.roll(odd, 64, 1)))
            second.append(jnp.where(low, pltpu.roll(even, 64, 1), odd))
            weight.append(wo[side * 4 + (xx + 4 - turns[turn]) % 4].reshape(128, WIDE))
        heads = jnp.concatenate([jnp.concatenate(first, 1), jnp.concatenate(second, 1)], 0).astype(BF)
        coarse_next = coarse_next + mm(heads, jnp.concatenate(weight, 0))
    upsampled = mm(coarse_next.astype(BF), wup[...])
    sent_by(back_s.at[0], ret_s)
    wait_sent()
    result = base + gain * upsampled
    stacked = jnp.concatenate([result[:, ab * 256 : ab * 256 + 256] for ab in range(4)], 0)
    upper = stacked.astype(BF)
    lower = (stacked - upper.astype(F32)).astype(BF)
    out_ref[...] = (mm(unshuffle, upper) + mm(unshuffle, lower)).reshape(32, 8, 256)


def shards(
    noisy_image,
    time_index,
    solver_index,
    time_gains,
    pixel_qkv,
    pixel_out,
    coarse_gains,
    coarse_qkv,
    coarse_out,
    upsample_weight,
    skip_gain,
    solver_table,
):
    vmem = pl.BlockSpec(memory_space=pltpu.VMEM)
    smem = pl.BlockSpec(memory_space=pltpu.SMEM)
    hbm = pl.BlockSpec(memory_space=pltpu.HBM)
    dma = pltpu.SemaphoreType.DMA
    return pl.pallas_call(
        kernel,
        out_shape=jax.ShapeDtypeStruct((32, 8, 256), F32),
        in_specs=[smem] * 2 + [hbm] * 10,
        out_specs=vmem,
        scratch_shapes=[
            pltpu.VMEM((32, 8, 256), BF),
            pltpu.VMEM((2, 32), F32),
            pltpu.VMEM((32, 256), F32),
            pltpu.VMEM((256, 768), BF),
            pltpu.VMEM((256, 256), BF),
            pltpu.VMEM((32, WIDE), F32),
            pltpu.VMEM((256,), F32),
            pltpu.VMEM((320, 256), BF),
            pltpu.VMEM((160, 256), BF),
            pltpu.VMEM((160, 256), BF),
            pltpu.VMEM((128, 256), BF),
            pltpu.VMEM((128, 256), BF),
            pltpu.VMEM((320, 512), BF),
            pltpu.VMEM((320, 512), BF),
            pltpu.VMEM((256, 256), BF),
            pltpu.VMEM((64, WIDE), BF),
            pltpu.VMEM((64, WIDE), BF),
            pltpu.VMEM((64, WIDE), BF),
            pltpu.VMEM((2, 4, 2, 64, WIDE), BF),
            pltpu.VMEM((192, WIDE), BF),
            pltpu.VMEM((256, WIDE), BF),
            pltpu.VMEM((8, 2, 64, WIDE), BF),
            pltpu.VMEM((WIDE, WIDE), BF),
            pltpu.VMEM((2, 4, 2, 64, 128), BF),
            pltpu.VMEM((2, 4, 2, 64, 128), BF),
            pltpu.VMEM((2, 4, 2, 64, 128), BF),
            pltpu.VMEM((4, 4, 32, 128), BF),
            pltpu.VMEM((4, 4, 32, 128), BF),
            dma((8,)),
            dma((8,)),
            dma((2,)),
            dma((CHUNKS,)),
            dma((1,)),
            dma((CHUNKS,)),
            dma((1,)),
            dma((CHUNKS,)),
            dma((2,)),
            dma((CHUNKS,)),
            dma((1,)),
            dma((CHUNKS,)),
            dma((1,)),
            dma((1,)),
            dma((1,)),
            dma((1,)),
            dma((1,)),
            dma((1,)),
            dma((1,)),
            dma((1,)),
            dma((2,)),
            dma((2,)),
            dma((1,)),
            dma((4,)),
            dma((10,)),
        ],
        compiler_params=pltpu.CompilerParams(
            collective_id=0, has_side_effects=True, vmem_limit_bytes=48 * 1024 * 1024
        ),
        cost_estimate=pl.CostEstimate(flops=2_000_000_000, bytes_accessed=8_000_000, transcendentals=1_300_000),
    )(
        time_index,
        solver_index,
        *(
            pltpu.with_memory_space_constraint(array, pltpu.HBM)
            for array in (
                noisy_image,
                solver_table.T,
                time_gains,
                pixel_qkv,
                pixel_out,
                coarse_gains,
                skip_gain,
                coarse_qkv.reshape(coarse_qkv.shape[0], coarse_qkv.shape[2]).T,
                coarse_out,
                upsample_weight,
            )
        ),
    )


def solution(mesh):
    placed = (
        P("row", "col", None),
        P(),
        P(),
        P(),
        P(),
        P(),
        P(),
        P(None, "row", None),
        P("row", None),
        P(),
        P(),
        P(),
    )
    return jax.shard_map(
        shards, mesh=mesh, in_specs=placed, out_specs=P("row", "col", None), check_vma=False
    )
```

time: 473 us -> 67.1 us (0.14)
  the two profiles are of different devices: /device:TPU:9 before, /device:TPU:1 now
where the time goes in v1:
time: 67.1 us; the launch traced here: 66.9 us
  Pallas kernels  64.9 us (97%)
  between operations  1.3 us (2%)
  local copies, waits for them, and re-layouts  0.71 us (1%)
    pallas_call x1, Pallas kernels, shards(): pl.pallas_call(kernel, out_shape=jax.ShapeDtypeStruct((32, 8, 256), F32),...  64.9 us

profile of v1, /device:TPU:1, one launch (start us, length us, event | category | flops | bytes accessed | tf_op | source)
XLA Modules:
  0.0 66.9 jit_solution(54989634209744167)
XLA Ops:
  1.3 64.9 %shard_map.118 = f32[32,8,256]{2,1,0:T(8,128)S(1)} custom-call(s32[1]{0:T(128)S(6)} %copy.14.time_ref, s32[1]{0:T(128)S(6)} %copy.15.step_ref, bf16[32,8,256]{2,1,0:T(8,128)(2,1)} %noisy_hbm.1, f32[2,32]{1,0:T(2,128)} %bitcast.5, f32[32,256]{1,0:T(8,128)} %gains_hbm.1, bf16[256,768]{1,0:T(8,128)(2,1)} %qkv_hbm.1, bf16[256,256]{1,0:T(8,128)(2,1)} %pout_hbm.1, ...), custom_call_target="tpu_custom_call" | custom-call | flops 2000000000 | bytes 8000000 | tf_op jit(solution)/shard_map/pallas_call | solution.py:561
  66.2 0.7 %copy.16 = f32[32,8,256]{2,1,0:T(8,128)} copy(f32[32,8,256]{2,1,0:T(8,128)S(1)} %shard_map.118) | data formatting | bytes 524288

commit v2 on v1

--- a/solution.py
+++ b/solution.py
@@ -72,14 +72,19 @@
     own,
     tok,
     wt,
+    wt_other,
     w3,
     wo,
     wup,
     asked_all,
     keys_all,
     values_all,
+    proj_s,
+    proj_r,
     ret_s,
     ret_r,
+    share_s,
+    share_r,
     halo_s,
     halo_r,
     z_s,
@@ -100,28 +105,29 @@
     w2_r,
     w3_s,
     w3_r,
-    w4_s,
-    w4_r,
+    wt_s,
+    wt_r,
+    share_sems,
     back_s,
     back_r,
     local,
 ):
     row, col = lax.axis_index("row"), lax.axis_index("col")
-    half, xx, core = row // 8, (row // 2) % 4, row % 2
-    yy = col % 4
-    group = row // 2
-    far_col = jnp.where(col >= 16, col - 16, col + 16)
-    far_row = jnp.where(row >= 8, row - 8, row + 8)
+    half, xx, core = row >> 3, (row >> 1) & 3, row & 1
+    yy = col & 3
+    group = row >> 1
+    far_col = (col + 16) & 31
+    far_row = (row + 8) & 15
     sibling = row + 1 - 2 * core
 
     fourth = jnp.where(row == 8, 0, 3)
     third = 3 - fourth
 
     def x_row(shift):
-        return half * 8 + ((xx + shift) % 4) * 2 + core
+        return half * 8 + ((xx + shift) & 3) * 2 + core
 
     def y_col(shift):
-        return col - yy + (yy + shift) % 4
+        return col - yy + ((yy + shift) & 3)
 
     def remote(src, dst, send, recv, where):
         return pltpu.make_async_remote_copy(
@@ -177,19 +183,11 @@
         partners = partners + flag.astype(jnp.int32)
 
     quarter = pl.ds(pl.multiple_of(yy * 16, 16), 16)
-    own_quarter = wo.at[group, core, quarter]
-    quarter = pl.ds(pl.multiple_of(yy * 16, 16), 16)
-    own_quarter = wo.at[group, core, quarter]
-    own_block = wo.at[group, core]
+    own_quarter = wo.at[group, quarter]
+    own_block = wo.at[group]
     load_wo = load(cout_hbm, own_block, 0)
     load_gains = load(gains_hbm, gains_ref, 4)
     load_qkv = load(qkv_hbm, qkv_ref, 5)
-    load_pout = load(pout_hbm, pout_ref, 6)
-    load_cgains = load(cgains_hbm, cgains_ref, 7)
-    load_wt = load(cqkv_hbm, wt, 1)
-    load_skip = load(skip_hbm, skip_ref, 8)
-    load_solver = load(solver_hbm, solver_ref, 9)
-    load_up = load(up_hbm, wup, 2)
 
     load_noisy.wait()
     tile = noisy_ref[...].astype(F32).reshape(256, 256)
@@ -235,13 +233,20 @@
             dst = halo[d][1]
             dst[...] = jnp.zeros(dst.shape, BF)
 
+    load_pout = load(pout_hbm, pout_ref, 6)
+    load_cgains = load(cgains_hbm, cgains_ref, 7)
+    load_wt = load(cqkv_hbm, wt, 1)
+    load_skip = load(skip_hbm, skip_ref, 8)
+    load_solver = load(solver_hbm, solver_ref, 9)
+    load_up = load(up_hbm, wup, 2)
+
     load_wo.wait()
     send(own_quarter, own_quarter, w1_s.at[0], w1_r.at[0], (far_row, far_col))
     sent_by(w1_s.at[0], own_quarter)
+    three = pl.ds(0, 3)
     for shift in (1, 2, 3):
         send(own_block, own_block, wx_s.at[0], wx_r.at[0], (x_row(shift), col))
-    three = pl.ds(0, 3)
-    sent_by(wx_s.at[0], wo.at[three, core])
+    sent_by(wx_s.at[0], wo.at[three])
 
     load_gains.wait()
     scales = pick(gains_ref[...], time_ref[0])
@@ -263,6 +268,8 @@
             noisy_m[block * 16 : block * 16 + 16, ab * 256 : ab * 256 + 256] = noisy_qb[at : at + 16]
 
     load_wt.wait()
+    send(wt, wt_other, wt_s.at[0], wt_r.at[0], (sibling, col))
+    sent_by(wt_s.at[0], wt)
     w3[0:64, :] = (wt[0:64, :].astype(F32) * 0.125).astype(BF)
     w3[64:192, :] = wt[64:192, :]
     w3[192:256, :] = jnp.zeros((64, WIDE), BF)
@@ -344,7 +351,25 @@
     def part(k):
         return pl.ds(k * PER, PER)
 
+    far_blocks = pl.ds(pl.multiple_of(4 - half * 4, 4), 4)
+
+    def weights_x():
+        ref = wo.at[far_row >> 1, quarter]
+        arrive(ref, w1_r.at[0], w1_s.at[0])
+        for shift in (1, 2, 3):
+            send(ref, ref, w2_s.at[0], w2_r.at[0], (x_row(shift), col))
+        sent_by(w2_s.at[0], wo.at[three, quarter])
+
+    def weights_y():
+        arrive(wo.at[three, quarter], w2_r.at[0], w2_s.at[0])
+        ref = wo.at[far_blocks, quarter]
+        for shift in (1, 2, 3):
+            send(ref, ref, w3_s.at[0], w3_r.at[0], (row, y_col(shift)))
+        sent_by(w3_s.at[0], wo.at[far_blocks, pl.ds(0, 48)])
+
     for k in range(CHUNKS):
+        if k == 3:
+            weights_x()
         if k < 2:
             window_block(k, k + 1)
         else:
@@ -354,7 +379,7 @@
         for t, target in enumerate((row, far_row)):
             send(
                 own.at[part(k)],
-                tok.at[half, xx, core, part(k)],
+                tok.at[half, xx >> 1, xx & 1, part(k)],
                 z_s.at[t],
                 z_r.at[k],
                 (target, far_col),
@@ -362,97 +387,72 @@
     for t in range(2):
         sent_by(z_s.at[t], own)
 
-    near_blocks = pl.ds(pl.multiple_of(half * 4, 4), 4)
-    far_blocks = pl.ds(pl.multiple_of(4 - half * 4, 4), 4)
-
-    def weights_x():
-        ref = wo.at[far_row // 2, core, quarter]
-        arrive(ref, w1_r.at[0], w1_s.at[0])
-        for shift in (1, 2, 3):
-            send(ref, ref, w2_s.at[0], w2_r.at[0], (x_row(shift), col))
-        sent_by(w2_s.at[0], wo.at[three, core, quarter])
-
-    def weights_y():
-        arrive(wo.at[three, core, quarter], w2_r.at[0], w2_s.at[0])
-        ref = wo.at[far_blocks, core, quarter]
-        for shift in (1, 2, 3):
-            send(ref, ref, w3_s.at[0], w3_r.at[0], (row, y_col(shift)))
-        sent_by(w3_s.at[0], wo.at[far_blocks, core, pl.ds(0, 48)])
-
-    def weights_near():
-        arrive(wo.at[three, core], wx_r.at[0], wx_s.at[0])
-        ref = wo.at[near_blocks, core]
-        send(ref, ref, w4_s.at[0], w4_r.at[0], (sibling, col))
-        sent_by(w4_s.at[0], ref)
-
-    def weights_far():
-        arrive(wo.at[far_blocks, core, pl.ds(0, 48)], w3_r.at[0], w3_s.at[0])
-        ref = wo.at[far_blocks, core]
-        send(ref, ref, w4_s.at[1], w4_r.at[1], (sibling, col))
-        sent_by(w4_s.at[1], ref)
-
-    def blocks(shift, k, which=core):
-        return tok.at[:, (xx + shift) % 4, which, part(k)]
+    def blocks(shift, k):
+        at = (xx + shift) & 3
+        return tok.at[:, at >> 1, at & 1, part(k)]
 
     def one(side, shift, k):
-        return tok.at[side, (xx + shift) % 4, core, part(k)]
-
-    def to_sibling(shift, k):
-        ref = blocks(shift, k)
-        send(ref, ref, sib_s.at[0], sib_r.at[k], (sibling, col))
+        at = (xx + shift) & 3
+        return tok.at[side, at >> 1, at & 1, part(k)]
 
     def gather(k):
         ref = blocks(0, k)
         arrive(ref, z_r.at[k], z_s.at[0])
         send(ref, ref, xr_s.at[0], xr_r.at[k], (x_row(1), col))
         send(ref, ref, xl_s.at[0], xl_r.at[k], (x_row(3), col))
-        to_sibling(0, k)
 
     def relay(k):
         arrive(blocks(3, k), xr_r.at[k], xr_s.at[0])
         ref = one(0, 3, k)
         send(ref, ref, xf_s.at[0], xf_r.at[k], (x_row(1), col))
-        to_sibling(3, k)
         arrive(blocks(1, k), xl_r.at[k], xl_s.at[0])
         ref = one(1, 1, k)
         send(ref, ref, xf_s.at[1], xf_r.at[k], (x_row(3), col))
-        to_sibling(1, k)
 
     def finish(k):
         arrive(blocks(2, k), xf_r.at[k], xf_s.at[0])
-        to_sibling(2, k)
-
-    def from_sibling(k):
-        arrive(tok.at[:, :, 1 - core, part(k)], sib_r.at[k], sib_s.at[0])
-
-    left = iota((16 * PER, 128), 1) < 64
-
-    def project(k):
-        tokens = tok[:, :, :, k * PER : (k + 1) * PER, :].reshape(16 * PER, WIDE)
-        result = nt(tokens, w3[...])
+
+    left = iota((8 * PER, 128), 1) < 64
+
+    def keep_proj(result, which, k):
         both, value = result[:, 0:128], result[:, 128:256]
         for ref, array in (
             (asked_all, jnp.where(left, both, 0.0)),
             (keys_all, pltpu.roll(both, 64, 1)),
             (values_all, jnp.where(left, value, 1.0)),
         ):
-            ref[:, :, :, k * PER : (k + 1) * PER, :] = array.astype(BF).reshape(2, 4, 2, PER, 128)
-
-    weights_x()
+            ref[:, :, which, k * PER : (k + 1) * PER, :] = array.astype(BF).reshape(2, 4, PER, 128)
+
+    def project(k):
+        tokens = tok[:, :, :, k * PER : (k + 1) * PER, :].reshape(8 * PER, WIDE)
+        result = nt(tokens, w3[...])
+        proj_s[k] = result[:, 256:512].astype(BF)
+        send(proj_s.at[k], proj_r.at[k], sib_s.at[0], sib_r.at[k], (sibling, col))
+        keep_proj(result[:, 0:256], core, k)
+
+    def from_sibling(k):
+        arrive(proj_r.at[k], sib_r.at[k], sib_s.at[0])
+        keep_proj(proj_r[k].astype(F32), 1 - core, k)
+
+    weights_y()
+    arrive(wt_other, wt_r.at[0], wt_s.at[0])
+    w3[256:320, :] = (wt_other[0:64, :].astype(F32) * 0.125).astype(BF)
+    w3[320:448, :] = wt_other[64:192, :]
+    w3[448:512, :] = jnp.zeros((64, WIDE), BF)
+
     gather(0)
-    weights_y()
     relay(0)
     for k in range(1, CHUNKS):
         gather(k)
         finish(k - 1)
         relay(k)
-        if k == 2:
-            weights_near()
-        from_sibling(k - 1)
         project(k - 1)
+        if k > 1:
+            from_sibling(k - 2)
     finish(CHUNKS - 1)
+    project(CHUNKS - 1)
+    from_sibling(CHUNKS - 2)
     from_sibling(CHUNKS - 1)
-    project(CHUNKS - 1)
 
     low = iota((32, 128), 1) < 64
     keys = keys_all[...].reshape(WIDE, 128)
@@ -461,14 +461,13 @@
     turns = (2, 1, 3, 0)
 
     def score(turn):
-        return nt(asked_all[:, (xx + turns[turn]) % 4].reshape(256, 128), keys)
-
-    whole = tok.at[:, xx, core]
+        return nt(asked_all[:, ((xx + turns[turn]) & 3)].reshape(256, 128), keys)
+
     for sem in (xr_s.at[0], xl_s.at[0]):
-        sent_by(sem, whole)
+        sent_by(sem, tok.at[:, 0, 0])
     for side in range(2):
-        sent_by(xf_s.at[side], tok.at[side, xx, core])
-    sent_by(sib_s.at[0], tok.at[:, :, core])
+        sent_by(xf_s.at[side], tok.at[side, 0, 0])
+    sent_by(sib_s.at[0], proj_s)
 
     scores = score(0)
     for turn in range(4):
@@ -479,19 +478,11 @@
         for which in range(4):
             at = 64 * which
             packed = jnp.where(low, mixed[at : at + 32], pltpu.roll(mixed[at + 32 : at + 64], 64, 1))
-            ret_s[turn, which] = packed.astype(BF)
-        for which in range(4):
-            target = (which // 2) * 8 + ((xx + turns[turn]) % 4) * 2 + which % 2
-            send(
-                ret_s.at[turn, which],
-                ret_r.at[turn, 2 * half + core],
-                back_s.at[0],
-                back_r.at[turn],
-                (target, far_col),
-            )
+            ret_s[turn, which // 2, which % 2] = packed.astype(BF)
+        for side in range(2):
+            target = side * 8 + ((xx + turns[turn]) & 3) * 2 + core
+            send(ret_s.at[turn, side], ret_r.at[turn, half], back_s.at[0], back_r.at[turn], (target, far_col))
         scores = following
-
-    weights_far()
 
     load_up.wait()
     load_skip.wait()
@@ -509,8 +500,8 @@
     spot = jnp.where((block == 1) | (block == 2), block - 1, jnp.where(block == third, 2, 3))
     source = (2 * (r & 1) + (c & 1)) * 64 + spot * 16 + ((r >> 1) & 3) * 4 + (c >> 1)
     unshuffle = (iota((256, 256), 1) == source).astype(F32).astype(BF)
-    arrive(wo.at[near_blocks, 1 - core], w4_r.at[0], w4_s.at[0])
-    arrive(wo.at[far_blocks, 1 - core], w4_r.at[1], w4_s.at[1])
+    arrive(wo.at[three], wx_r.at[0], wx_s.at[0])
+    arrive(wo.at[far_blocks, pl.ds(0, 48)], w3_r.at[0], w3_s.at[0])
     for d in range(8):
 
         @pl.when(there[d])
@@ -519,19 +510,33 @@
 
     wait_sent()
 
-    coarse_next = pixels
-    for turn in range(4):
-        arrive(ret_r.at[turn], back_r.at[turn], back_s.at[0])
-        first, second, weight = [], [], []
-        for side in range(2):
-            even, odd = ret_r[turn, 2 * side].astype(F32), ret_r[turn, 2 * side + 1].astype(F32)
-            first.append(jnp.where(low, even, pltpu.roll(odd, 64, 1)))
-            second.append(jnp.where(low, pltpu.roll(even, 64, 1), odd))
-            weight.append(wo[side * 4 + (xx + 4 - turns[turn]) % 4].reshape(128, WIDE))
-        heads = jnp.concatenate([jnp.concatenate(first, 1), jnp.concatenate(second, 1)], 0).astype(BF)
-        coarse_next = coarse_next + mm(heads, jnp.concatenate(weight, 0))
+    def head_rows(turn, which):
+        even, odd = ret_r[turn, 0, which].astype(F32), ret_r[turn, 1, which].astype(F32)
+        first = jnp.where(low, even, pltpu.roll(odd, 64, 1))
+        second = jnp.where(low, pltpu.roll(even, 64, 1), odd)
+        return jnp.concatenate([first, second], 0).astype(BF)
+
+    shares = [None, None]
+    for couple in range(2):
+        weight = []
+        for turn in (2 * couple, 2 * couple + 1):
+            arrive(ret_r.at[turn], back_r.at[turn], back_s.at[0])
+            from_x = (xx + 4 - turns[turn]) & 3
+            weight += [wo[from_x], wo[4 + from_x]]
+        weight = jnp.concatenate(weight, 0)
+        for at, which in enumerate((1 - core, core)):
+            heads = jnp.concatenate([head_rows(2 * couple, which), head_rows(2 * couple + 1, which)], 1)
+            share = mm(heads, weight)
+            shares[at] = share if couple == 0 else shares[at] + share
+            if couple == 1 and at == 0:
+                share_s[...] = shares[0].astype(BF)
+                send(share_s, share_r, share_sems.at[0], share_sems.at[1], (sibling, col))
+    coarse_next = pixels + shares[1]
+    arrive(share_r, share_sems.at[1], share_sems.at[0])
+    coarse_next = coarse_next + share_r[...].astype(F32)
     upsampled = mm(coarse_next.astype(BF), wup[...])
     sent_by(back_s.at[0], ret_s)
+    sent_by(share_sems.at[0], share_s)
     wait_sent()
     result = base + gain * upsampled
     stacked = jnp.concatenate([result[:, ab * 256 : ab * 256 + 256] for ab in range(4)], 0)
@@ -582,16 +587,21 @@
             pltpu.VMEM((64, WIDE), BF),
             pltpu.VMEM((64, WIDE), BF),
             pltpu.VMEM((64, WIDE), BF),
-            pltpu.VMEM((2, 4, 2, 64, WIDE), BF),
+            pltpu.VMEM((2, 2, 2, 64, WIDE), BF),
             pltpu.VMEM((192, WIDE), BF),
-            pltpu.VMEM((256, WIDE), BF),
-            pltpu.VMEM((8, 2, 64, WIDE), BF),
+            pltpu.VMEM((192, WIDE), BF),
+            pltpu.VMEM((512, WIDE), BF),
+            pltpu.VMEM((8, 64, WIDE), BF),
             pltpu.VMEM((WIDE, WIDE), BF),
             pltpu.VMEM((2, 4, 2, 64, 128), BF),
             pltpu.VMEM((2, 4, 2, 64, 128), BF),
             pltpu.VMEM((2, 4, 2, 64, 128), BF),
-            pltpu.VMEM((4, 4, 32, 128), BF),
-            pltpu.VMEM((4, 4, 32, 128), BF),
+            pltpu.VMEM((CHUNKS, 8 * PER, 256), BF),
+            pltpu.VMEM((CHUNKS, 8 * PER, 256), BF),
+            pltpu.VMEM((4, 2, 2, 32, 128), BF),
+            pltpu.VMEM((4, 2, 2, 32, 128), BF),
+            pltpu.VMEM((64, WIDE), BF),
+            pltpu.VMEM((64, WIDE), BF),
             dma((8,)),
             dma((8,)),
             dma((2,)),
@@ -612,7 +622,8 @@
             dma((1,)),
             dma((1,)),
             dma((1,)),
-            dma((2,)),
+            dma((1,)),
+            dma((1,)),
             dma((2,)),
             dma((1,)),
             dma((4,)),

time: 67.1 us -> 66.8 us (level)
  the two profiles are of different devices: /device:TPU:1 before, /device:TPU:9 now
where the time goes in v2:
time: 66.8 us; the launch traced here: 66.6 us
  Pallas kernels  64.6 us (97%)
  between operations  1.3 us (2%)
  local copies, waits for them, and re-layouts  0.71 us (1%)
    pallas_call x1, Pallas kernels, shards(): pl.pallas_call(kernel, out_shape=jax.ShapeDtypeStruct((32, 8, 256), F32),...  64.6 us

profile of v2, /device:TPU:9, one launch (start us, length us, event | category | flops | bytes accessed | tf_op | source)
XLA Modules:
  0.0 66.6 jit_solution(13956481071088358525)
XLA Ops:
  1.3 64.6 %shard_map.118 = f32[32,8,256]{2,1,0:T(8,128)S(1)} custom-call(s32[1]{0:T(128)S(6)} %copy.14.time_ref, s32[1]{0:T(128)S(6)} %copy.15.step_ref, bf16[32,8,256]{2,1,0:T(8,128)(2,1)} %noisy_hbm.1, f32[2,32]{1,0:T(2,128)} %bitcast.5, f32[32,256]{1,0:T(8,128)} %gains_hbm.1, bf16[256,768]{1,0:T(8,128)(2,1)} %qkv_hbm.1, bf16[256,256]{1,0:T(8,128)(2,1)} %pout_hbm.1, ...), custom_call_target="tpu_custom_call" | custom-call | flops 2000000000 | bytes 8000000 | tf_op jit(solution)/shard_map/pallas_call | solution.py:566
  65.9 0.7 %copy.16 = f32[32,8,256]{2,1,0:T(8,128)} copy(f32[32,8,256]{2,1,0:T(8,128)S(1)} %shard_map.118) | data formatting | bytes 524288

commit v3 on v2

--- a/solution.py
+++ b/solution.py
@@ -99,8 +99,6 @@
     sib_r,
     w1_s,
     w1_r,
-    wx_s,
-    wx_r,
     w2_s,
     w2_r,
     w3_s,
@@ -184,8 +182,7 @@
 
     quarter = pl.ds(pl.multiple_of(yy * 16, 16), 16)
     own_quarter = wo.at[group, quarter]
-    own_block = wo.at[group]
-    load_wo = load(cout_hbm, own_block, 0)
+    load_wo = load(cout_hbm.at[quarter], own_quarter, 0)
     load_gains = load(gains_hbm, gains_ref, 4)
     load_qkv = load(qkv_hbm, qkv_ref, 5)
 
@@ -245,8 +242,7 @@
     sent_by(w1_s.at[0], own_quarter)
     three = pl.ds(0, 3)
     for shift in (1, 2, 3):
-        send(own_block, own_block, wx_s.at[0], wx_r.at[0], (x_row(shift), col))
-    sent_by(wx_s.at[0], wo.at[three])
+        send(own_quarter, own_quarter, w2_s.at[0], w2_r.at[0], (x_row(shift), col))
 
     load_gains.wait()
     scales = pick(gains_ref[...], time_ref[0])
@@ -351,23 +347,24 @@
     def part(k):
         return pl.ds(k * PER, PER)
 
-    far_blocks = pl.ds(pl.multiple_of(4 - half * 4, 4), 4)
-
     def weights_x():
         ref = wo.at[far_row >> 1, quarter]
         arrive(ref, w1_r.at[0], w1_s.at[0])
         for shift in (1, 2, 3):
-            send(ref, ref, w2_s.at[0], w2_r.at[0], (x_row(shift), col))
-        sent_by(w2_s.at[0], wo.at[three, quarter])
-
-    def weights_y():
-        arrive(wo.at[three, quarter], w2_r.at[0], w2_s.at[0])
-        ref = wo.at[far_blocks, quarter]
+            send(ref, ref, w2_s.at[1], w2_r.at[1], (x_row(shift), col))
+
+    def weights_y(far):
+        arrive(wo.at[three, quarter], w2_r.at[far], w2_s.at[far])
+        sent_by(w2_s.at[far], wo.at[three, quarter])
+        side = 1 - half if far else half
+        ref = wo.at[pl.ds(pl.multiple_of(side * 4, 4), 4), quarter]
         for shift in (1, 2, 3):
-            send(ref, ref, w3_s.at[0], w3_r.at[0], (row, y_col(shift)))
-        sent_by(w3_s.at[0], wo.at[far_blocks, pl.ds(0, 48)])
+            send(ref, ref, w3_s.at[far], w3_r.at[far], (row, y_col(shift)))
+        sent_by(w3_s.at[far], wo.at[pl.ds(0, 4), pl.ds(0, 48)])
 
     for k in range(CHUNKS):
+        if k == 2:
+            weights_y(0)
         if k == 3:
             weights_x()
         if k < 2:
@@ -434,7 +431,7 @@
         arrive(proj_r.at[k], sib_r.at[k], sib_s.at[0])
         keep_proj(proj_r[k].astype(F32), 1 - core, k)
 
-    weights_y()
+    weights_y(1)
     arrive(wt_other, wt_r.at[0], wt_s.at[0])
     w3[256:320, :] = (wt_other[0:64, :].astype(F32) * 0.125).astype(BF)
     w3[320:448, :] = wt_other[64:192, :]
@@ -500,8 +497,8 @@
     spot = jnp.where((block == 1) | (block == 2), block - 1, jnp.where(block == third, 2, 3))
     source = (2 * (r & 1) + (c & 1)) * 64 + spot * 16 + ((r >> 1) & 3) * 4 + (c >> 1)
     unshuffle = (iota((256, 256), 1) == source).astype(F32).astype(BF)
-    arrive(wo.at[three], wx_r.at[0], wx_s.at[0])
-    arrive(wo.at[far_blocks, pl.ds(0, 48)], w3_r.at[0], w3_s.at[0])
+    for far in range(2):
+        arrive(wo.at[pl.ds(0, 4), pl.ds(0, 48)], w3_r.at[far], w3_s.at[far])
     for d in range(8):
 
         @pl.when(there[d])
@@ -616,12 +613,10 @@
             dma((CHUNKS,)),
             dma((1,)),
             dma((1,)),
-            dma((1,)),
-            dma((1,)),
-            dma((1,)),
-            dma((1,)),
-            dma((1,)),
-            dma((1,)),
+            dma((2,)),
+            dma((2,)),
+            dma((2,)),
+            dma((2,)),
             dma((1,)),
             dma((1,)),
             dma((2,)),

time: 66.8 us -> 66.4 us (level)
  no operation moved by 1% of the time
where the time goes in v3:
time: 66.4 us; the launch traced here: 66.2 us
  Pallas kernels  64.2 us (97%)
  between operations  1.3 us (2%)
  local copies, waits for them, and re-layouts  0.71 us (1%)
    pallas_call x1, Pallas kernels, shards(): pl.pallas_call(kernel, out_shape=jax.ShapeDtypeStruct((32, 8, 256), F32),...  64.2 us

profile of v3, /device:TPU:9, one launch (start us, length us, event | category | flops | bytes accessed | tf_op | source)
XLA Modules:
  0.0 66.2 jit_solution(14315177082428206501)
XLA Ops:
  1.3 64.2 %shard_map.118 = f32[32,8,256]{2,1,0:T(8,128)S(1)} custom-call(s32[1]{0:T(128)S(6)} %copy.14.time_ref, s32[1]{0:T(128)S(6)} %copy.15.step_ref, bf16[32,8,256]{2,1,0:T(8,128)(2,1)} %noisy_hbm.1, f32[2,32]{1,0:T(2,128)} %bitcast.5, f32[32,256]{1,0:T(8,128)} %gains_hbm.1, bf16[256,768]{1,0:T(8,128)(2,1)} %qkv_hbm.1, bf16[256,256]{1,0:T(8,128)(2,1)} %pout_hbm.1, ...), custom_call_target="tpu_custom_call" | custom-call | flops 2000000000 | bytes 8000000 | tf_op jit(solution)/shard_map/pallas_call | solution.py:563
  65.5 0.7 %copy.16 = f32[32,8,256]{2,1,0:T(8,128)} copy(f32[32,8,256]{2,1,0:T(8,128)S(1)} %shard_map.118) | data formatting | bytes 524288

commit v4 on v3

--- a/solution.py
+++ b/solution.py
@@ -64,6 +64,7 @@
     rr,
     pack_l,
     pack_r,
+    relayed,
     kv_c,
     kv_e,
     query,
@@ -87,6 +88,9 @@
     share_r,
     halo_s,
     halo_r,
+    seam_s,
+    seam_r,
+    hand_s,
     z_s,
     z_r,
     xr_s,
@@ -163,12 +167,19 @@
     there = []
     for down, right in DIRS:
         r, c = row + down, col + right
-        there.append((r >= 0) & (r < ROWS) & (c >= 0) & (c < COLS))
-    for d, (down, right) in enumerate(DIRS):
-
-        @pl.when(there[d])
+        inside = (r >= 0) & (r < ROWS) & (c >= 0) & (c < COLS)
+        there.append(inside & (row != 7) if down == 1 else inside)
+
+        @pl.when(inside & (row != 8) if down == -1 else inside)
         def _():
             greet((row + down, col + right))
+
+    for right in (-1, 0, 1):
+
+        @pl.when((row == 0) & (far_col + right >= 0) & (far_col + right < COLS))
+        def _():
+            greet((7, far_col + right))
+
 
     greet((row, far_col))
     greet((far_row, far_col))
@@ -177,7 +188,8 @@
         greet((row, y_col(shift)))
     greet((sibling, col))
     partners = 2 + 6 + 1
-    for flag in there:
+    seam = [(row == 7) & (col + right >= 0) & (col + right < COLS) for right in (0, 1, -1)]
+    for flag in there + seam:
         partners = partners + flag.astype(jnp.int32)
 
     quarter = pl.ds(pl.multiple_of(yy * 16, 16), 16)
@@ -218,6 +230,25 @@
         @pl.when(there[d])
         def _():
             halo_copy(d).start()
+
+    slots = (relayed.at[0:32], relayed.at[32:48], relayed.at[48:64])
+
+    def seam_copy(piece):
+        src = (cc.at[256:288], pack_r.at[112:128], pack_l.at[112:128])[piece]
+        c = col + (0, 1, -1)[piece]
+        where = (0, (c + 16) & 31)
+        return remote(src, slots[piece], seam_s.at[piece], seam_r.at[piece], where)
+
+    def hand_copy(piece):
+        d = (1, 7, 6)[piece]
+        return remote(slots[piece], halo[d][1], hand_s.at[piece], halo_r.at[d], (8, far_col))
+
+    handed = [(row == 0) & (far_col + right >= 0) & (far_col + right < COLS) for right in (0, -1, 1)]
+    for piece in range(3):
+
+        @pl.when(seam[piece])
+        def _():
+            seam_copy(piece).start()
 
     from_there = []
     for down, right in DIRS:
@@ -277,6 +308,13 @@
 
     def edge_kv(array):
         return mm(norm(array.astype(F32), scales), qkv_ref[:, 256:768]).astype(BF)
+
+    for piece in range(3):
+
+        @pl.when(handed[piece])
+        def _():
+            arrive(slots[piece], seam_r.at[piece], seam_s.at[piece])
+            hand_copy(piece).start()
 
     halo_wait(2, True)
     halo_wait(3, True)
@@ -363,10 +401,12 @@
         sent_by(w3_s.at[far], wo.at[pl.ds(0, 4), pl.ds(0, 48)])
 
     for k in range(CHUNKS):
+        if k == 1:
+            weights_y(0)
         if k == 2:
-            weights_y(0)
+            weights_x()
         if k == 3:
-            weights_x()
+            weights_y(1)
         if k < 2:
             window_block(k, k + 1)
         else:
@@ -431,7 +471,6 @@
         arrive(proj_r.at[k], sib_r.at[k], sib_s.at[0])
         keep_proj(proj_r[k].astype(F32), 1 - core, k)
 
-    weights_y(1)
     arrive(wt_other, wt_r.at[0], wt_s.at[0])
     w3[256:320, :] = (wt_other[0:64, :].astype(F32) * 0.125).astype(BF)
     w3[320:448, :] = wt_other[64:192, :]
@@ -504,6 +543,16 @@
         @pl.when(there[d])
         def _():
             halo_copy(d).wait_send()
+
+    for piece in range(3):
+
+        @pl.when(seam[piece])
+        def _():
+            seam_copy(piece).wait_send()
+
+        @pl.when(handed[piece])
+        def _():
+            hand_copy(piece).wait_send()
 
     wait_sent()
 
@@ -578,6 +627,7 @@
             pltpu.VMEM((160, 256), BF),
             pltpu.VMEM((128, 256), BF),
             pltpu.VMEM((128, 256), BF),
+            pltpu.VMEM((64, 256), BF),
             pltpu.VMEM((320, 512), BF),
             pltpu.VMEM((320, 512), BF),
             pltpu.VMEM((256, 256), BF),
@@ -601,6 +651,9 @@
             pltpu.VMEM((64, WIDE), BF),
             dma((8,)),
             dma((8,)),
+            dma((3,)),
+            dma((3,)),
+            dma((3,)),
             dma((2,)),
             dma((CHUNKS,)),
             dma((1,)),

time: 66.4 us -> 66.6 us (level)
  no operation moved by 1% of the time
where the time goes in v4:
time: 66.6 us; the launch traced here: 66.2 us
  Pallas kernels  64.2 us (96%)
  between operations  1.3 us (2%)
  local copies, waits for them, and re-layouts  0.71 us (1%)
    pallas_call x1, Pallas kernels, shards(): pl.pallas_call(kernel, out_shape=jax.ShapeDtypeStruct((32, 8, 256), F32),...  64.2 us

profile of v4, /device:TPU:9, one launch (start us, length us, event | category | flops | bytes accessed | tf_op | source)
XLA Modules:
  0.0 66.2 jit_solution(3712847596583483648)
XLA Ops:
  1.3 64.2 %shard_map.118 = f32[32,8,256]{2,1,0:T(8,128)S(1)} custom-call(s32[1]{0:T(128)S(6)} %copy.14.time_ref, s32[1]{0:T(128)S(6)} %copy.15.step_ref, bf16[32,8,256]{2,1,0:T(8,128)(2,1)} %noisy_hbm.1, f32[2,32]{1,0:T(2,128)} %bitcast.5, f32[32,256]{1,0:T(8,128)} %gains_hbm.1, bf16[256,768]{1,0:T(8,128)(2,1)} %qkv_hbm.1, bf16[256,256]{1,0:T(8,128)(2,1)} %pout_hbm.1, ...), custom_call_target="tpu_custom_call" | custom-call | flops 2000000000 | bytes 8000000 | tf_op jit(solution)/shard_map/pallas_call | solution.py:612
  65.5 0.7 %copy.16 = f32[32,8,256]{2,1,0:T(8,128)} copy(f32[32,8,256]{2,1,0:T(8,128)S(1)} %shard_map.118) | data formatting | bytes 524288

commit v5 on v4

--- a/solution.py
+++ b/solution.py
@@ -164,6 +164,14 @@
     def greet(where):
         pl.semaphore_signal(barrier, inc=1, device_id=where, device_id_type=MESH)
 
+    greet((row, far_col))
+    greet((far_row, far_col))
+    for right in (-1, 0, 1):
+
+        @pl.when((row == 0) & (far_col + right >= 0) & (far_col + right < COLS))
+        def _():
+            greet((7, far_col + right))
+
     there = []
     for down, right in DIRS:
         r, c = row + down, col + right
@@ -174,15 +182,6 @@
         def _():
             greet((row + down, col + right))
 
-    for right in (-1, 0, 1):
-
-        @pl.when((row == 0) & (far_col + right >= 0) & (far_col + right < COLS))
-        def _():
-            greet((7, far_col + right))
-
-
-    greet((row, far_col))
-    greet((far_row, far_col))
     for shift in (1, 2, 3):
         greet((x_row(shift), col))
         greet((row, y_col(shift)))

time: 66.6 us -> 67.2 us (level)
  Pallas kernels: 64.2 us -> 65 us
    pallas_call x1, Pallas kernels: 64.2 us -> 65 us  [shards(): pl.pallas_call(kernel, out_shape=jax.ShapeDtypeStruct((32, 8, 256), F32),...]
where the time goes in v5:
time: 67.2 us; the launch traced here: 67 us
  Pallas kernels  65 us (97%)
  between operations  1.3 us (2%)
  local copies, waits for them, and re-layouts  0.71 us (1%)
    pallas_call x1, Pallas kernels, shards(): pl.pallas_call(kernel, out_shape=jax.ShapeDtypeStruct((32, 8, 256), F32),...  65 us

profile of v5, /device:TPU:9, one launch (start us, length us, event | category | flops | bytes accessed | tf_op | source)
XLA Modules:
  0.0 67.0 jit_solution(12708056034140010132)
XLA Ops:
  1.3 65.0 %shard_map.118 = f32[32,8,256]{2,1,0:T(8,128)S(1)} custom-call(s32[1]{0:T(128)S(6)} %copy.14.time_ref, s32[1]{0:T(128)S(6)} %copy.15.step_ref, bf16[32,8,256]{2,1,0:T(8,128)(2,1)} %noisy_hbm.1, f32[2,32]{1,0:T(2,128)} %bitcast.5, f32[32,256]{1,0:T(8,128)} %gains_hbm.1, bf16[256,768]{1,0:T(8,128)(2,1)} %qkv_hbm.1, bf16[256,256]{1,0:T(8,128)(2,1)} %pout_hbm.1, ...), custom_call_target="tpu_custom_call" | custom-call | flops 2000000000 | bytes 8000000 | tf_op jit(solution)/shard_map/pallas_call | solution.py:611
  66.3 0.7 %copy.16 = f32[32,8,256]{2,1,0:T(8,128)} copy(f32[32,8,256]{2,1,0:T(8,128)S(1)} %shard_map.118) | data formatting | bytes 524288
